TPU v7x, 32 devices: a whole 2x2x4 slice. The times are simulated.
32 devices in a mesh: dp: 8 (over z, x), tensor: 4 (over y, core).
Axes of the slice: x: 2, y: 2, z: 4, core: 2. Of those that a mesh axis runs over, the one named last changes fastest.
Arguments:
- hidden_in: bfloat16 [8192, 1152], P(('dp', 'tensor')), may hold values from -6 to 6
- picture_ids: int32 [8192], P('dp'), may hold values from -1 to 9, as said below
- norm1_gain: float32 [1152], replicated, may hold values from 0.5 to 1.5
- norm1_bias: float32 [1152], replicated, may hold values from -1.75 to 1.75
- w_qkv: bfloat16 [3, 1152, 1152], P(None, None, 'tensor'), may hold values from -1 to 1
- qv_bias: float32 [2, 1152], P(None, 'tensor'), may hold values from -3 to 3
- w_out: bfloat16 [1152, 1152], P('tensor'), may hold values from -0.75 to 0.75
- out_bias: float32 [1152], replicated, may hold values from -1.75 to 1.75
- norm2_gain: float32 [1152], replicated, may hold values from 0.5 to 1.5
- norm2_bias: float32 [1152], replicated, may hold values from -1.75 to 1.75
- w_up: bfloat16 [1152, 4304], P(None, 'tensor'), may hold values from -0.1875 to 0.1875
- up_bias: float32 [4304], P('tensor'), may hold values from -3 to 3
- w_down: bfloat16 [4304, 1152], P('tensor'), may hold values from -0.125 to 0.125
- down_bias: float32 [1152], replicated, may hold values from -1.75 to 1.75
- cotangent: bfloat16 [8192, 1152], P(('dp', 'tensor')), may hold values from -6 to 6
Outputs:
- hidden_out: bfloat16 [8192, 1152], P(('dp', 'tensor'))
- grad_in: bfloat16 [8192, 1152], P(('dp', 'tensor'))
- grad_qkv: float32 [3, 1152, 1152], P(None, 'dp', 'tensor')
- grad_out: float32 [1152, 1152], P('tensor', 'dp')
- grad_up: float32 [1152, 4304], P('dp', 'tensor')
- grad_down: float32 [4304, 1152], P('tensor', 'dp')
- grad_qv_bias: float32 [2, 1152], P(None, 'tensor')
- grad_up_bias: float32 [4304], P('tensor')
- grad_shared: float32 [6, 1152], replicated
- head_maxima: float32 [16], P('tensor')
- scaled_qk: bfloat16 [2, 1152, 1152], P(None, None, 'tensor')
- scaled_query_bias: float32 [1152], P('tensor')
Inputs may be any that keep to these rules, and one draw needn't show every extreme that they name: `picture_ids`: each aligned row of 1024 tokens holds whole pictures of 100 to 1024 patches one after another, numbered from 0 within the row, then padding with id -1; some row holds a single picture of 1024 patches, and some other row holds 10 pictures of 100 patches.
All inputs are finite; a program needn't handle non-finite values.
Results may differ from a plain program's by a relative error of at most 0.014.
Values may be sent and summed in bfloat16 or wider, within the bound.
No kernel may reach another device: no remote copies, remote signals or barrier semaphores. Data moves between devices by JAX's collectives and lax.ppermute only.
A program may use at most 192 MiB of HBM per device.

v0:
```python
import jax
import jax.numpy as jnp
from jax import lax
from jax.sharding import PartitionSpec as P

HEAD_DIM = 72
PACK = 1024
QBLOCK = 512
CLIP_LIMIT = 9
eps_norm = 1e-06
neg_fill = -1e30


def normalize(values_in, gain, shift):
    row_mean = jnp.mean(values_in, axis=-1, keepdims=True)
    centred = values_in - row_mean
    variance = jnp.mean(centred * centred, axis=-1, keepdims=True)
    inverse = lax.rsqrt(variance + eps_norm)
    unit_rows = centred * inverse
    return (unit_rows * gain + shift, unit_rows, inverse)


def norm_back(grad_rows, unit_rows, inverse, gain):
    scaled = grad_rows * gain
    return inverse * (
        scaled
        - jnp.mean(scaled, axis=-1, keepdims=True)
        - unit_rows * jnp.mean(scaled * unit_rows, axis=-1, keepdims=True)
    )


def gelu_tanh(inputs):
    return jax.nn.gelu(inputs, approximate=True)


def local(
    hidden_in,
    picture_ids,
    norm1_gain,
    norm1_bias,
    w_qkv,
    qv_bias,
    w_out,
    out_bias,
    norm2_gain,
    norm2_bias,
    w_up,
    up_bias,
    w_down,
    down_bias,
    cotangent,
):
    group_rows = picture_ids.shape[0]
    row_count = group_rows // PACK
    head_width = w_qkv.shape[2]
    local_heads = head_width // HEAD_DIM
    score_scale = HEAD_DIM ** (-0.5)
    block_count = PACK // QBLOCK
    block_shape = (row_count, block_count, QBLOCK, local_heads, HEAD_DIM)
    row_shape = (row_count, PACK, local_heads, HEAD_DIM)
    source = hidden_in.astype(jnp.float32)
    normed_a, unit_a, inverse_a = normalize(source, norm1_gain, norm1_bias)
    whole_a = lax.all_gather(normed_a.astype(jnp.bfloat16), "tensor", axis=0, tiled=True)
    projected = jnp.einsum("td,cde->cte", whole_a, w_qkv, preferred_element_type=jnp.float32)
    queries = (projected[0] + qv_bias[0]).astype(jnp.bfloat16)
    key_rows = projected[1].astype(jnp.bfloat16)
    values = (projected[2] + qv_bias[1]).astype(jnp.bfloat16)
    query_blocks = queries.reshape(block_shape)
    key_heads = key_rows.reshape(row_shape)
    value_heads = values.reshape(row_shape)
    row_ids = picture_ids.reshape(row_count, PACK)

    def attend_row(parts_in):
        row_q, row_k, row_v, ids_row = parts_in
        block_ids = ids_row.reshape(block_count, QBLOCK)

        def attend_block(block_in):
            block_q, query_ids = block_in
            scores = (
                jnp.einsum("qhd,khd->hqk", block_q, row_k, preferred_element_type=jnp.float32)
                * score_scale
            )
            allowed = query_ids[:, None] == ids_row[None, :]
            scores = jnp.where(allowed[None], scores, neg_fill)
            row_top = jnp.max(scores, axis=2, keepdims=True)
            weights = jnp.exp(scores - row_top)
            row_sum = jnp.sum(weights, axis=2, keepdims=True)
            prob_rows = (weights / row_sum).astype(jnp.bfloat16)
            attended = jnp.einsum(
                "hqk,khd->qhd", prob_rows, row_v, preferred_element_type=jnp.float32
            )
            return (
                attended.astype(jnp.bfloat16),
                (row_top + jnp.log(row_sum))[:, :, 0],
                jnp.max(row_top[:, :, 0], axis=1),
            )

        return lax.map(attend_block, (row_q, block_ids))

    attended, log_total, block_top = lax.map(
        attend_row, (query_blocks, key_heads, value_heads, row_ids)
    )
    flat_att = attended.reshape(group_rows, head_width)
    branch_a = lax.psum_scatter(
        jnp.dot(flat_att, w_out, preferred_element_type=jnp.float32),
        "tensor",
        scatter_dimension=0,
        tiled=True,
    )
    residual = source + branch_a + out_bias
    normed_b, unit_b, inverse_b = normalize(residual, norm2_gain, norm2_bias)
    whole_b = lax.all_gather(normed_b.astype(jnp.bfloat16), "tensor", axis=0, tiled=True)
    pre_act = jnp.dot(whole_b, w_up, preferred_element_type=jnp.float32) + up_bias
    activated = gelu_tanh(pre_act).astype(jnp.bfloat16)
    branch_b = lax.psum_scatter(
        jnp.dot(activated, w_down, preferred_element_type=jnp.float32).astype(jnp.bfloat16),
        "tensor",
        scatter_dimension=0,
        tiled=True,
    ).astype(jnp.float32)
    hidden_out = (residual + branch_b + down_bias).astype(jnp.bfloat16)
    head_maxima = lax.pmax(jnp.max(block_top, axis=(0, 1)), "dp")
    limit = jnp.float32(CLIP_LIMIT)
    factor = jnp.sqrt(limit / jnp.maximum(head_maxima, limit))
    column = jnp.repeat(factor, HEAD_DIM)
    scaled_qk = (w_qkv[:2].astype(jnp.float32) * column).astype(jnp.bfloat16)
    scaled_query_bias = qv_bias[0] * column
    whole_grad = lax.all_gather(cotangent, "tensor", axis=0, tiled=True)
    grad_act = jnp.einsum("td,fd->tf", whole_grad, w_down, preferred_element_type=jnp.float32)
    grad_pre = jax.vjp(gelu_tanh, pre_act)[1](grad_act)[0].astype(jnp.bfloat16)
    grad_down = jnp.einsum("tf,td->fd", activated, whole_grad, preferred_element_type=jnp.float32)
    grad_up = jnp.einsum("td,tf->df", whole_b, grad_pre, preferred_element_type=jnp.float32)
    grad_up_bias = jnp.sum(grad_pre, axis=0, dtype=jnp.float32)
    grad_norm_b = lax.psum_scatter(
        jnp.einsum("tf,df->td", grad_pre, w_up, preferred_element_type=jnp.float32),
        "tensor",
        scatter_dimension=0,
        tiled=True,
    )
    grad_top = cotangent.astype(jnp.float32)
    grad_resid = grad_top + norm_back(grad_norm_b, unit_b, inverse_b, norm2_gain)
    grad_branch = grad_resid.astype(jnp.bfloat16)
    whole_branch = lax.all_gather(grad_branch, "tensor", axis=0, tiled=True)
    grad_out = jnp.einsum("te,td->ed", flat_att, whole_branch, preferred_element_type=jnp.float32)
    grad_att = jnp.einsum(
        "td,ed->te", whole_branch, w_out, preferred_element_type=jnp.float32
    ).astype(jnp.bfloat16)

    def back_row(parts_in):
        row_q, row_k, row_v, ids_row, row_grad, row_lse = parts_in
        block_ids = ids_row.reshape(block_count, QBLOCK)

        def back_block(state_in, block_in):
            key_grad, value_grad = state_in
            block_q, query_ids, block_grad, block_lse = block_in
            scores = (
                jnp.einsum("qhd,khd->hqk", block_q, row_k, preferred_element_type=jnp.float32)
                * score_scale
            )
            allowed = query_ids[:, None] == ids_row[None, :]
            scores = jnp.where(allowed[None], scores, neg_fill)
            prob_full = jnp.exp(scores - block_lse[:, :, None])
            grad_probs = jnp.einsum(
                "qhd,khd->hqk", block_grad, row_v, preferred_element_type=jnp.float32
            )
            inner = jnp.sum(prob_full * grad_probs, axis=2, keepdims=True)
            grad_scores = (prob_full * (grad_probs - inner)).astype(jnp.bfloat16)
            query_grad = (
                jnp.einsum("hqk,khd->qhd", grad_scores, row_k, preferred_element_type=jnp.float32)
                * score_scale
            )
            key_grad = (
                key_grad
                + jnp.einsum(
                    "hqk,qhd->khd", grad_scores, block_q, preferred_element_type=jnp.float32
                )
                * score_scale
            )
            value_grad = value_grad + jnp.einsum(
                "hqk,qhd->khd",
                prob_full.astype(jnp.bfloat16),
                block_grad,
                preferred_element_type=jnp.float32,
            )
            return ((key_grad, value_grad), query_grad.astype(jnp.bfloat16))

        zero_rows = jnp.zeros(row_k.shape, jnp.float32)
        (key_grad, value_grad), query_grad = lax.scan(
            back_block, (zero_rows, zero_rows), (row_q, block_ids, row_grad, row_lse)
        )
        return (query_grad, key_grad.astype(jnp.bfloat16), value_grad.astype(jnp.bfloat16))

    query_grad, key_grad, value_grad = lax.map(
        back_row,
        (query_blocks, key_heads, value_heads, row_ids, grad_att.reshape(block_shape), log_total),
    )
    grad_stack = jnp.stack(
        [
            query_grad.reshape(group_rows, head_width),
            key_grad.reshape(group_rows, head_width),
            value_grad.reshape(group_rows, head_width),
        ]
    )
    grad_qkv = jnp.einsum("td,cte->cde", whole_a, grad_stack, preferred_element_type=jnp.float32)
    grad_qv_bias = jnp.stack(
        [
            jnp.sum(grad_stack[0], axis=0, dtype=jnp.float32),
            jnp.sum(grad_stack[2], axis=0, dtype=jnp.float32),
        ]
    )
    grad_norm_a = lax.psum_scatter(
        jnp.einsum("cte,cde->td", grad_stack, w_qkv, preferred_element_type=jnp.float32),
        "tensor",
        scatter_dimension=0,
        tiled=True,
    )
    grad_in = (grad_resid + norm_back(grad_norm_a, unit_a, inverse_a, norm1_gain)).astype(
        jnp.bfloat16
    )
    grad_qkv, grad_out, grad_up, grad_down = (
        lax.psum_scatter(grad_qkv, "dp", scatter_dimension=1, tiled=True),
        lax.psum_scatter(grad_out, "dp", scatter_dimension=1, tiled=True),
        lax.psum_scatter(grad_up, "dp", scatter_dimension=0, tiled=True),
        lax.psum_scatter(grad_down, "dp", scatter_dimension=1, tiled=True),
    )
    grad_qv_bias, grad_up_bias = lax.psum((grad_qv_bias, grad_up_bias), "dp")
    shared_part = jnp.stack(
        [
            jnp.sum(grad_norm_a * unit_a, axis=0),
            jnp.sum(grad_norm_a, axis=0),
            jnp.sum(grad_resid, axis=0),
            jnp.sum(grad_norm_b * unit_b, axis=0),
            jnp.sum(grad_norm_b, axis=0),
            jnp.sum(grad_top, axis=0),
        ]
    )
    grad_shared = lax.psum(shared_part, ("dp", "tensor"))
    return (
        hidden_out,
        grad_in,
        grad_qkv,
        grad_out,
        grad_up,
        grad_down,
        grad_qv_bias,
        grad_up_bias,
        grad_shared,
        head_maxima,
        scaled_qk,
        scaled_query_bias,
    )


def solution(mesh):
    return jax.shard_map(
        local,
        mesh=mesh,
        in_specs=(
            P(("dp", "tensor"), None),
            P("dp"),
            P(),
            P(),
            P(None, None, "tensor"),
            P(None, "tensor"),
            P("tensor", None),
            P(),
            P(),
            P(),
            P(None, "tensor"),
            P("tensor"),
            P("tensor", None),
            P(),
            P(("dp", "tensor"), None),
        ),
        out_specs=(
            P(("dp", "tensor"), None),
            P(("dp", "tensor"), None),
            P(None, "dp", "tensor"),
            P("tensor", "dp"),
            P("dp", "tensor"),
            P("tensor", "dp"),
            P(None, "tensor"),
            P("tensor"),
            P(),
            P("tensor"),
            P(None, None, "tensor"),
            P("tensor"),
        ),
        check_vma=False,
    )
```

profile of v0, /device:TPU:0, one launch (start us, length us, event | category | flops | bytes accessed | tf_op | source)
XLA Modules:
  0.0 802.8 jit_solution(1162977882640721757)
XLA Ops:
  12.5 26.6 %all-gather.5.cloned.1.call-done = bf16[1024,1152]{1,0:T(8,128)(2,1)} async-done(((bf16[256,1152]{1,0:T(8,128)(2,1)}), bf16[1024,1152]{1,0:T(8,128)(2,1)}) %all-gather.5.cloned.1.call-update) | async-done | bytes 2359312 | tf_op jit(solution)/shard_map/all_gather | solution.py:63
  39.2 4.7 fusion.54
  45.6 3.2 squeeze.52
  48.8 2.3 add_convert_fusion.2
  53.0 20.3 %while.51 = (s32[]{:T(128)}, bf16[2,512,4,72]{1,3,2,0:T(8,128)(2,1)}, f32[2,4,512]{2,1,0:T(4,128)S(1)}, f32[2,4]{1,0:T(2,128)S(1)}, s32[2,512]{1,0:T(2,128)S(1)}...) while((s32[]{:T(128)}, ...), condition=%wide.region_6.7_spmd, body=%wide.region_2.6_spmd.sunk | while | flops 631912448 | bytes 36186380 | solution.py:98
  53.4 2.8 fusion.132
  56.2 2.9 fusion.133
  59.2 3.1 fusion.134
  63.6 2.8 fusion.132
  66.4 2.9 fusion.133
  69.3 3.1 fusion.134
  76.0 3.6 fusion.82
  80.5 47.2 %reduce-scatter.11.cloned.1.call-done = f32[256,1152]{1,0:T(8,128)} async-done(((f32[1024,1152]{1,0:T(8,128)}), f32[256,1152]{1,0:T(8,128)}) %reduce-scatter.11.cloned.1.call-update) | async-done | bytes 1179664 | tf_op jit(solution)/shard_map/reduce_scatter | solution.py:104
  131.7 21.7 %all-gather.9.cloned.1.call-done = bf16[1024,1152]{1,0:T(8,128)(2,1)} async-done(((bf16[256,1152]{1,0:T(8,128)(2,1)}), bf16[1024,1152]{1,0:T(8,128)(2,1)}) %all-gather.9.cloned.1.call-update) | async-done | bytes 2359312 | tf_op jit(solution)/shard_map/all_gather | solution.py:128
  153.5 7.5 fusion.83
  161.0 18.6 %all-gather.7.cloned.1.call-done = bf16[1024,1152]{1,0:T(8,128)(2,1)} async-done(((bf16[256,1152]{1,0:T(8,128)(2,1)}), bf16[1024,1152]{1,0:T(8,128)(2,1)}) %all-gather.7.cloned.1.call-update) | async-done | bytes 2359312 | tf_op jit(solution)/shard_map/all_gather | solution.py:112
  179.6 9.9 %convert_reduce_fusion = (f32[1076]{0:T(1024)}, bf16[1024,1076]{0,1:T(8,128)(2,1)S(1)}, f32[1024,1076]{0,1:T(8,128)}) fusion(f32[1024,1076]{0,1:T(8,128)} %fusion.83, f32[1076]{0:T(1024)S(1)} %copy-done.48, bf16[1024,1152]{1,0:T(8,128)(2,1)} %all-gather.7.cloned.1.call-done, bf16[1152,1076]{0,1:T(8,128)(2,1)S(1)} %copy-done), kind=kOutput, calls=%fused_computation.63 | convolution fusion | flops 2563943424 | bytes 15865248 | tf_op jit(solution)/shard_map/dot_general | solution.py:113
  190.9 5.2 fusion.84
  197.8 7.5 convolution_convert_fusion
  205.4 38.8 %reduce-scatter.15.cloned.1.call-done = f32[256,1152]{1,0:T(8,128)} async-done(((f32[1024,1152]{1,0:T(8,128)}), f32[256,1152]{1,0:T(8,128)}) %reduce-scatter.15.cloned.1.call-update) | async-done | bytes 1179664 | tf_op jit(solution)/shard_map/reduce_scatter | solution.py:134
  244.1 2.4 multiply_reduce_fusion.1
  246.5 33.1 %reduce-scatter.13.cloned.1.call-done = bf16[256,1152]{1,0:T(8,128)(2,1)} async-done(((bf16[1024,1152]{1,0:T(8,128)(2,1)}), bf16[256,1152]{1,0:T(8,128)(2,1)}) %reduce-scatter.13.cloned.1.call-update) | async-done | bytes 589840 | tf_op jit(solution)/shard_map/reduce_scatter | solution.py:115
  279.6 3.6 fusion.77
  284.5 23.9 %all-gather.11.cloned.1.call-done = bf16[1024,1152]{1,0:T(8,128)(2,1)} async-done(((bf16[256,1152]{1,0:T(8,128)(2,1)}), bf16[1024,1152]{1,0:T(8,128)(2,1)}) %all-gather.11.cloned.1.call-update) | async-done | bytes 2359312 | tf_op jit(solution)/shard_map/all_gather | solution.py:143
  308.4 3.6 convolution_convert_fusion.1
  316.0 25.9 %while.52 = (s32[]{:T(128)}, f32[1024,4,72]{0,2,1:T(8,128)S(1)}, f32[1024,4,72]{0,2,1:T(8,128)}, bf16[2,512,4,72]{1,3,2,0:T(8,128)(2,1)}, bf16[2,512,4,72]{1,3,2...) while((s32[]{:T(128)}, f32[1024,4,72]{0,2,1:T(8,128)S(1)}, ...), condition=%wide.region_16.17_spmd.clone, body=%wide.region_14.16_spmd.clone.sunk | while | flops 1543698432 | bytes 91916632 | solution.py:188
  317.8 2.6 fusion.146
  320.5 3.3 multiply_reduce_fusion.7
  323.8 2.4 multiply_convert_fusion.6
  330.6 2.6 fusion.146
  333.3 3.3 multiply_reduce_fusion.7
  336.6 2.4 multiply_convert_fusion.6
  344.6 6.3 convolution_bitcast_fusion.1
  350.9 8.6 %copy.41 = f32[3,1152,288]{2,0,1:T(4,128)} copy(f32[3,1152,288]{1,2,0:T(8,128)} %convolution_bitcast_fusion.1) | data formatting | bytes 7962624
  359.5 9.0 %reshape.211 = f32[1152,864]{1,0:T(8,128)} reshape(f32[1152,3,288]{2,1,0:T(4,128)} %bitcast.143) | data formatting | bytes 7962624
  370.1 6.3 convolution_bitcast_fusion
  376.5 8.6 %fusion.76 = f32[1076,1152]{0,1:T(8,128)} fusion(bf16[1024,1152]{1,0:T(8,128)(2,1)} %all-gather.9.cloned.1.call-done, f32[1024,1076]{0,1:T(8,128)} %get-tuple-element.355), kind=kOutput, calls=%fused_computation.124 | convolution fusion | flops 2548518912 | bytes 11724800 | tf_op jit(solution)/shard_map/tf,td->fd/dot_general | solution.py:131
  385.4 8.0 fusion.86
  394.5 4.4 fusion.85
  399.1 22.0 %pmax.7 = f32[4]{0:T(128)S(1)} all-reduce(f32[4]{0:T(128)S(1)} %reduce_max.27), channel_id=1, replica_groups=mesh['dp'=8,'tensor'=4] {'dp'}, use_global_device_ids=true, to_apply=%region_37.38 | all-reduce | flops 4 | bytes 32 | tf_op jit(solution)/shard_map/pmax | solution.py:122
  423.7 34.2 %all-reduce = (f32[2,288]{1,0:T(2,128)}, f32[1076]{0:T(1024)}) all-reduce(f32[2,288]{1,0:T(2,128)S(1)} %pad_maximum_fusion.3, f32[1076]{0:T(1024)S(1)} %copy-done.43), channel_id=1, replica_groups=mesh['dp'=8,'tensor'=4] {'dp'}, use_global_device_ids=true, to_apply=%region_26.27 | all-reduce | flops 1652 | bytes 13216 | tf_op jit(solution)/shard_map/psum | solution.py:226
  457.9 2.4 reshape.212
  462.5 44.9 %reduce-scatter.17.cloned.1.call-done = f32[256,1152]{1,0:T(8,128)} async-done(((f32[1024,1152]{1,0:T(8,128)}), f32[256,1152]{1,0:T(8,128)}) %reduce-scatter.17.cloned.1.call-update) | async-done | bytes 1179664 | tf_op jit(solution)/shard_map/reduce_scatter | solution.py:211
  509.3 42.9 %psum.23 = f32[6,1152]{1,0:T(8,128)} all-reduce(f32[6,1152]{1,0:T(8,128)S(1)} %stack.43), channel_id=1, replica_groups=mesh['dp'=8,'tensor'=4] {'dp','tensor'}, use_global_device_ids=true, to_apply=%region_35.36 | all-reduce | flops 6912 | bytes 55296 | tf_op jit(solution)/shard_map/psum | solution.py:237
  552.2 2.9 fusion.69
  555.1 62.2 %reduce-scatter.23.cloned.1.call-done = f32[1076,144]{0,1:T(8,128)} async-done(((f32[1076,1152]{0,1:T(8,128)}), f32[1076,144]{0,1:T(8,128)}) %reduce-scatter.23.cloned.1.call-update) | async-done | bytes 619792 | tf_op jit(solution)/shard_map/reduce_scatter | solution.py:224
  617.3 108.1 %reduce-scatter.21.cloned.1.call-done = f32[144,1076]{1,0:T(8,128)} async-done(((f32[1152,1076]{1,0:T(8,128)}), f32[144,1076]{1,0:T(8,128)}) %reduce-scatter.21.cloned.1.call-update) | async-done | bytes 619792 | tf_op jit(solution)/shard_map/reduce_scatter | solution.py:223
  725.4 70.3 %reduce-scatter.19.cloned.1.call-done = f32[288,144]{0,1:T(8,128)} async-done(((f32[288,1152]{0,1:T(8,128)}), f32[288,144]{0,1:T(8,128)}) %reduce-scatter.19.cloned.1.call-update) | async-done | bytes 165904 | tf_op jit(solution)/shard_map/reduce_scatter | solution.py:222
  (219 shorter events, 47.9 us)
Async XLA Ops:
  7.2 172.5 %copy-start = (bf16[1152,1076]{0,1:T(8,128)(2,1)S(1)}, bf16[1152,1076]{0,1:T(8,128)(2,1)}, u32[]{:S(2)}) copy-start(bf16[1152,1076]{0,1:T(8,128)(2,1)} %param.29) | copy-start | bytes 7437316
  7.2 5.1 copy-start.27
  7.2 5.1 copy-start.44
  7.2 32.0 %all-gather.5.cloned.1.call-start = ((), (), s32[]{:S(2)}) async-start(), calls=%async_computation.8 | async-start | bytes 2949120 | tf_op jit(solution)/shard_map/all_gather | solution.py:63
  8.6 30.5 %copy-start.34 = (f32[256]{0:T(256)}, f32[256]{0:T(256)S(1)}, u32[]{:S(2)}) copy-start(f32[256]{0:T(256)S(1)} %broadcast_multiply_fusion.5) | copy-start | bytes 3076
  10.0 29.2 %copy-start.38 = (f32[256]{0:T(256)}, f32[256]{0:T(256)S(1)}, u32[]{:S(2)}) copy-start(f32[256]{0:T(256)S(1)} %add_rsqrt_fusion.1) | copy-start | bytes 3076
  12.2 115.5 %reduce-scatter.11.cloned.1.call-start = ((), (), s32[]{:S(2)}) async-start(), calls=%async_computation.9 | async-start | bytes 5898240 | tf_op jit(solution)/shard_map/reduce_scatter | solution.py:104
  12.4 31.6 %copy-start.36 = (f32[288]{0:T(512)}, f32[288]{0:T(512)S(1)}, u32[]{:S(2)}) copy-start(f32[288]{0:T(512)S(1)} %get-tuple-element.296) | copy-start | bytes 3460
  56.2 2.9 copy-start.16
  66.4 2.9 copy-start.16
  73.3 6.3 copy-start.45
  79.7 48.0 %copy-start.40 = (f32[1152]{0:T(1024)S(1)}, f32[1152]{0:T(1024)}, u32[]{:S(2)}) copy-start(f32[1152]{0:T(1024)} %param.26) | copy-start | bytes 13828
  79.7 50.7 %copy-start.28 = (f32[1152]{0:T(1024)S(1)}, f32[1152]{0:T(1024)}, u32[]{:S(2)}) copy-start(f32[1152]{0:T(1024)} %param.27) | copy-start | bytes 13828
  79.7 50.7 %copy-start.41 = (f32[1152]{0:T(1024)S(1)}, f32[1152]{0:T(1024)}, u32[]{:S(2)}) copy-start(f32[1152]{0:T(1024)} %param.28) | copy-start | bytes 13828
  79.7 73.7 %all-gather.9.cloned.1.call-start = ((), (), s32[]{:S(2)}) async-start(), calls=%async_computation.12 | async-start | bytes 2949120 | tf_op jit(solution)/shard_map/all_gather | solution.py:128
  80.5 99.2 %all-gather.7.cloned.1.call-start = ((), (), s32[]{:S(2)}) async-start(), calls=%async_computation.10 | async-start | bytes 2949120 | tf_op jit(solution)/shard_map/all_gather | solution.py:112
  131.5 48.1 %copy-start.48 = (f32[1076]{0:T(1024)S(1)}, f32[1076]{0:T(1024)}, u32[]{:S(2)}) copy-start(f32[1076]{0:T(1024)} %param.30) | copy-start | bytes 12916
  131.5 112.6 %reduce-scatter.15.cloned.1.call-start = ((), (), s32[]{:S(2)}) async-start(), calls=%async_computation.13 | async-start | bytes 5898240 | tf_op jit(solution)/shard_map/reduce_scatter | solution.py:134
  196.1 83.5 %reduce-scatter.13.cloned.1.call-start = ((), (), s32[]{:S(2)}) async-start(), calls=%async_computation.11 | async-start | bytes 2949120 | tf_op jit(solution)/shard_map/reduce_scatter | solution.py:115
  205.3 38.8 %copy-start.4 = (f32[256,1152]{1,0:T(8,128)S(1)}, f32[256,1152]{1,0:T(8,128)}, u32[]{:S(2)}) copy-start(f32[256,1152]{1,0:T(8,128)} %copy-done.3) | copy-start | bytes 3538948
  205.3 74.3 %copy-start.42 = (f32[1152]{0:T(1024)S(1)}, f32[1152]{0:T(1024)}, u32[]{:S(2)}) copy-start(f32[1152]{0:T(1024)} %param.32) | copy-start | bytes 13828
  205.3 103.1 %all-gather.11.cloned.1.call-start = ((), (), s32[]{:S(2)}) async-start(), calls=%async_computation.14 | async-start | bytes 2949120 | tf_op jit(solution)/shard_map/all_gather | solution.py:143
  283.2 25.2 %copy-start.8 = (f32[256,1152]{1,0:T(8,128)}, f32[256,1152]{1,0:T(8,128)S(1)}, u32[]{:S(2)}) copy-start(f32[256,1152]{1,0:T(8,128)S(1)} %get-tuple-element.340) | copy-start | bytes 3538948
  284.2 173.7 %reduce-scatter.25.cloned.1.call-start = ((), (), s32[]{:S(2)}) async-start(), calls=%async_computation.19 | async-start | bytes 4644864
  312.0 4.0 copy-start.2
  320.5 3.3 copy-start.19
  333.3 3.3 copy-start.19
  342.0 8.9 %copy-start.23 = (bf16[1024,4,72]{0,2,1:T(8,128)(2,1)}, bf16[1024,4,72]{0,2,1:T(8,128)(2,1)S(1)}, u32[]{:S(2)}) copy-start(bf16[1024,4,72]{0,2,1:T(8,128)(2,1)S(1)} %convert_element_type.109) | copy-start | bytes 1769476
  344.4 6.5 copy-start.25
  344.6 6.4 copy-start.26
  368.5 138.9 %reduce-scatter.17.cloned.1.call-start = ((), (), s32[]{:S(2)}) async-start(), calls=%async_computation.15 | async-start | bytes 5898240 | tf_op jit(solution)/shard_map/reduce_scatter | solution.py:211
  376.5 240.9 %reduce-scatter.23.cloned.1.call-start = ((), (), s32[]{:S(2)}) async-start(), calls=%async_computation.18 | async-start | bytes 5971968 | tf_op jit(solution)/shard_map/reduce_scatter | solution.py:224
  385.2 340.2 %reduce-scatter.21.cloned.1.call-start = ((), (), s32[]{:S(2)}) async-start(), calls=%async_computation.17 | async-start | bytes 5971968 | tf_op jit(solution)/shard_map/reduce_scatter | solution.py:223
  393.4 5.6 copy-start.46
  393.5 27.8 %copy-start.37 = (f32[288]{0:T(512)S(1)}, f32[288]{0:T(512)}, u32[]{:S(2)}) copy-start(f32[288]{0:T(512)} %copy-done.36) | copy-start | bytes 3460
  393.5 402.3 %reduce-scatter.19.cloned.1.call-start = ((), (), s32[]{:S(2)}) async-start(), calls=%async_computation.16 | async-start | bytes 1990656 | tf_op jit(solution)/shard_map/reduce_scatter | solution.py:222
  399.0 24.2 %copy-start.31 = (f32[1152]{0:T(1024)S(1)}, f32[1152]{0:T(1024)}, u32[]{:S(2)}) copy-start(f32[1152]{0:T(1024)} %get-tuple-element.287) | copy-start | bytes 13828
  399.0 24.2 %copy-start.33 = (f32[1152]{0:T(1024)S(1)}, f32[1152]{0:T(1024)}, u32[]{:S(2)}) copy-start(f32[1152]{0:T(1024)} %get-tuple-element.339) | copy-start | bytes 13828
  399.0 24.2 %copy-start.32 = (f32[1152]{0:T(1024)S(1)}, f32[1152]{0:T(1024)}, u32[]{:S(2)}) copy-start(f32[1152]{0:T(1024)} %get-tuple-element.354) | copy-start | bytes 13828
  399.0 24.3 %copy-start.30 = (f32[1152]{0:T(1024)S(1)}, f32[1152]{0:T(1024)}, u32[]{:S(2)}) copy-start(f32[1152]{0:T(1024)} %get-tuple-element.293) | copy-start | bytes 13828
  399.0 24.3 %copy-start.12 = (bf16[2,512,4,72]{1,3,2,0:T(8,128)(2,1)S(1)}, bf16[2,512,4,72]{1,3,2,0:T(8,128)(2,1)}, u32[]{:S(2)}) copy-start(bf16[2,512,4,72]{1,3,2,0:T(8,128)(2,1)} %get-tuple-element.176) | copy-start | bytes 1769476
  399.0 24.6 %copy-start.43 = (f32[1076]{0:T(1024)S(1)}, f32[1076]{0:T(1024)}, u32[]{:S(2)}) copy-start(f32[1076]{0:T(1024)} %get-tuple-element.341) | copy-start | bytes 12916
  421.1 39.2 %copy-start.49 = (f32[4]{0:T(128)}, f32[4]{0:T(128)S(1)}, u32[]{:S(2)}) copy-start(f32[4]{0:T(128)S(1)} %pmax.7) | copy-start | bytes 52
  423.2 84.2 %copy-start.7 = (bf16[256,1152]{1,0:T(8,128)(2,1)S(1)}, bf16[256,1152]{1,0:T(8,128)(2,1)}, u32[]{:S(2)}) copy-start(bf16[256,1152]{1,0:T(8,128)(2,1)} %param.19) | copy-start | bytes 1769476
  423.2 84.2 %copy-start.29 = (f32[1152]{0:T(1024)S(1)}, f32[1152]{0:T(1024)}, u32[]{:S(2)}) copy-start(f32[1152]{0:T(1024)} %param.21) | copy-start | bytes 13828
  423.2 84.2 %copy-start.35 = (f32[256]{0:T(256)S(1)}, f32[256]{0:T(256)}, u32[]{:S(2)}) copy-start(f32[256]{0:T(256)} %copy-done.34) | copy-start | bytes 3076
  423.2 84.2 %copy-start.39 = (f32[256]{0:T(256)S(1)}, f32[256]{0:T(256)}, u32[]{:S(2)}) copy-start(f32[256]{0:T(256)} %copy-done.38) | copy-start | bytes 3076
  460.3 335.5 %copy-start.1 = (bf16[1152,1076]{0,1:T(8,128)(2,1)S(1)}, bf16[1152,1076]{0,1:T(8,128)(2,1)}, u32[]{:S(2)}) copy-start(bf16[1152,1076]{0,1:T(8,128)(2,1)} %param.29) | copy-start | bytes 7437316
  (24 other events, 42.1 us)
Sparse Core Ops, SparseCore 0:
  12.4 26.7 all-gather.4
  79.8 47.8 reduce-scatter.10
  129.4 24.0 all-gather.8
  155.5 24.0 all-gather.6
  196.2 47.8 reduce-scatter.14
  246.5 33.0 reduce-scatter.12
  284.3 24.0 all-gather.10
  368.6 88.3 reduce-scatter.24
  459.6 47.7 reduce-scatter.16
  511.8 105.4 reduce-scatter.22
  621.5 103.8 reduce-scatter.20
  729.7 65.9 reduce-scatter.18
where the time goes:
time: 812 us; the launch traced here: 803 us
  waiting for transfers between devices  496 us (61%)
  matrix products  107 us (13%)
  blocking collectives  99.1 us (12%)
  local copies, waits for them, and re-layouts  46 us (6%)
  other arithmetic  37.6 us (5%)
  between operations  14.9 us (2%)
    reduce_scatter x1, waiting for transfers between devices, local(): lax.psum_scatter(grad_up, 'dp', scatter_dimension=0, tiled=True)  108 us
    reduce_scatter x1, waiting for transfers between devices, local(): lax.psum_scatter(grad_out, 'dp', scatter_dimension=1, tiled=True)  70.3 us
    reduce_scatter x1, waiting for transfers between devices, local(): lax.psum_scatter(grad_down, 'dp', scatter_dimension=1, tiled=True)  62.2 us
    reduce_scatter x1, waiting for transfers between devices, local(): lax.psum_scatter(jnp.dot(flat_att, w_out, preferred_element_type=jnp.floa...  47.2 us
    reduce_scatter x1, waiting for transfers between devices, local(): lax.psum_scatter(jnp.einsum('cte,cde->td', grad_stack, w_qkv, preferred_e...  44.9 us
    psum x1, blocking collectives, local(): grad_shared = lax.psum(shared_part, ('dp', 'tensor'))  42.9 us
    reduce_scatter x1, waiting for transfers between devices, local(): lax.psum_scatter(jnp.einsum('tf,df->td', grad_pre, w_up, preferred_elemen...  38.8 us
    psum x1, blocking collectives, local(): grad_qv_bias, grad_up_bias = lax.psum((grad_qv_bias, grad_up_bias), 'dp')  34.2 us
  transfers between devices with their start and end apart: 12, of which 11 were waited for; matrix products, arithmetic and copies ran while one was open for 7% of the time, Pallas kernels for 0%

commit v1 on v0

--- a/solution.py
+++ b/solution.py
@@ -1,7 +1,9 @@
+import functools
 import jax
 import jax.numpy as jnp
 from jax import lax
 from jax.sharding import PartitionSpec as P
+from jax.lax import axis_index, axis_size, ppermute
 
 HEAD_DIM = 72
 PACK = 1024
@@ -9,6 +11,22 @@
 CLIP_LIMIT = 9
 eps_norm = 1e-06
 neg_fill = -1e30
+
+
+def block_draft(sheet, array_axis):
+    amount_of = axis_size("tensor")
+    crops = tuple(((t, (t + 1) % amount_of) for t in range(amount_of)))
+    v_next = [None] * amount_of
+    v_next[amount_of - 1] = sheet
+    for m in range(amount_of - 2, -1, -1):
+        v_next[m] = ppermute(v_next[m + 1], "tensor", crops)
+    now = jnp.concatenate(v_next, axis=array_axis)
+    everything = (axis_index("tensor") + 1) * sheet.shape[array_axis]
+    r2 = jnp.roll(now, everything, axis=array_axis)
+    return r2
+
+
+tokens_list = functools.partial(block_draft, array_axis=0)
 
 
 def normalize(values_in, gain, shift):
@@ -125,7 +143,7 @@
     column = jnp.repeat(factor, HEAD_DIM)
     scaled_qk = (w_qkv[:2].astype(jnp.float32) * column).astype(jnp.bfloat16)
     scaled_query_bias = qv_bias[0] * column
-    whole_grad = lax.all_gather(cotangent, "tensor", axis=0, tiled=True)
+    whole_grad = tokens_list(cotangent)
     grad_act = jnp.einsum("td,fd->tf", whole_grad, w_down, preferred_element_type=jnp.float32)
     grad_pre = jax.vjp(gelu_tanh, pre_act)[1](grad_act)[0].astype(jnp.bfloat16)
     grad_down = jnp.einsum("tf,td->fd", activated, whole_grad, preferred_element_type=jnp.float32)

time: 812 us -> 812 us (level)
  local copies, waits for them, and re-layouts: 46 us -> 57.8 us
  waiting for transfers between devices: 496 us -> 485 us
    ppermute x0 -> x3, waiting for transfers between devices: none -> 28.8 us  [block_draft(): v_next[m] = ppermute(v_next[m + 1], 'tensor', crops)]
    all_gather x1 -> x0, waiting for transfers between devices: 21.7 us -> none  [local(): whole_grad = lax.all_gather(cotangent, 'tensor', axis=0, tiled=True)]
    all_gather x1, waiting for transfers between devices: 18.6 us -> 0.01 us  [local(): lax.all_gather(normed_b.astype(jnp.bfloat16), 'tensor', axis=0, tiled=True)]
    unnamed x90 -> x101, local copies, waits for them, and re-layouts: 30.4 us -> 41.4 us
  transfers between devices with their start and end apart: 12 -> 14, of which waited for: 11 -> 11; matrix products, arithmetic and copies ran while one was open for 7% -> 8% of each run, Pallas kernels for 0% -> 0%
where the time goes in v1:
time: 812 us; the launch traced here: 802 us
  waiting for transfers between devices  485 us (60%)
  matrix products  105 us (13%)
  blocking collectives  99.2 us (12%)
  local copies, waits for them, and re-layouts  57.8 us (7%)
  other arithmetic  37.6 us (5%)
  between operations  14.6 us (2%)
    reduce_scatter x1, waiting for transfers between devices, local(): lax.psum_scatter(grad_up, 'dp', scatter_dimension=0, tiled=True)  108 us
    reduce_scatter x1, waiting for transfers between devices, local(): lax.psum_scatter(grad_out, 'dp', scatter_dimension=1, tiled=True)  70.1 us
    reduce_scatter x1, waiting for transfers between devices, local(): lax.psum_scatter(grad_down, 'dp', scatter_dimension=1, tiled=True)  62 us
    reduce_scatter x1, waiting for transfers between devices, local(): lax.psum_scatter(jnp.dot(flat_att, w_out, preferred_element_type=jnp.floa...  47.6 us
    reduce_scatter x1, waiting for transfers between devices, local(): lax.psum_scatter(jnp.einsum('cte,cde->td', grad_stack, w_qkv, preferred_e...  44.7 us
    psum x1, blocking collectives, local(): grad_shared = lax.psum(shared_part, ('dp', 'tensor'))  43 us
    unnamed x101, local copies, waits for them, and re-layouts  41.4 us
    reduce_scatter x1, waiting for transfers between devices, local(): lax.psum_scatter(jnp.einsum('tf,df->td', grad_pre, w_up, preferred_elemen...  40.4 us
  transfers between devices with their start and end apart: 14, of which 11 were waited for; matrix products, arithmetic and copies ran while one was open for 8% of the time, Pallas kernels for 0%

profile of v1, /device:TPU:0, one launch (start us, length us, event | category | flops | bytes accessed | tf_op | source)
XLA Modules:
  0.0 802.3 jit_solution(16639380123264990548)
XLA Ops:
  12.5 26.6 %all-gather.4.cloned.1.call-done = bf16[1024,1152]{1,0:T(8,128)(2,1)} async-done(((bf16[256,1152]{1,0:T(8,128)(2,1)}), bf16[1024,1152]{1,0:T(8,128)(2,1)}) %all-gather.4.cloned.1.call-update) | async-done | bytes 2359312 | tf_op jit(solution)/shard_map/all_gather | solution.py:81
  39.2 4.7 fusion.60
  45.6 3.2 squeeze.52
  48.8 2.3 add_convert_fusion.2
  53.0 20.3 %while.51 = (s32[]{:T(128)}, bf16[2,512,4,72]{1,3,2,0:T(8,128)(2,1)}, f32[2,4,512]{2,1,0:T(4,128)S(1)}, f32[2,4]{1,0:T(2,128)S(1)}, s32[2,512]{1,0:T(2,128)S(1)}...) while((s32[]{:T(128)}, ...), condition=%wide.region_6.7_spmd, body=%wide.region_2.6_spmd.sunk | while | flops 631912448 | bytes 36186380 | solution.py:116
  53.4 2.8 fusion.135
  56.2 2.9 fusion.136
  59.2 3.1 fusion.137
  63.6 2.8 fusion.135
  66.4 2.9 fusion.136
  69.3 3.1 fusion.137
  76.0 3.7 fusion.88
  80.1 47.6 %reduce-scatter.11.cloned.1.call-done = f32[256,1152]{1,0:T(8,128)} async-done(((f32[1024,1152]{1,0:T(8,128)}), f32[256,1152]{1,0:T(8,128)}) %reduce-scatter.11.cloned.1.call-update) | async-done | bytes 1179664 | tf_op jit(solution)/shard_map/reduce_scatter | solution.py:122
  131.7 9.6 %collective-permute-done.1 = bf16[256,1152]{1,0:T(8,128)(2,1)} collective-permute-done((bf16[256,1152]{1,0:T(8,128)(2,1)}, bf16[256,1152]{1,0:T(8,128)(2,1)}, u32[]{:S(2)}, u32[]{:S(2)}) %collective-permute-start.1) | collective-permute-done | bytes 589856 | tf_op jit(solution)/shard_map/ppermute | solution.py:22
  141.5 19.2 %collective-permute-done.2 = bf16[256,1152]{1,0:T(8,128)(2,1)} collective-permute-done((bf16[256,1152]{1,0:T(8,128)(2,1)}, bf16[256,1152]{1,0:T(8,128)(2,1)}, u32[]{:S(2)}, u32[]{:S(2)}) %collective-permute-start.2) | collective-permute-done | bytes 589856 | tf_op jit(solution)/shard_map/ppermute | solution.py:22
  174.1 5.5 convolution_add_fusion
  179.6 10.1 %convert_reduce_fusion = (f32[1076]{0:T(1024)}, bf16[1024,1076]{0,1:T(8,128)(2,1)S(1)}) fusion(f32[1024,1076]{0,1:T(8,128)S(1)} %convolution_add_fusion, bf16[1076,1152]{1,0:T(8,128)(2,1)S(1)} %copy-done, bf16[2048,1152]{1,0:T(8,128)(2,1)} %constant_dynamic-update-slice_fusion, s32[]{:T(128)S(6)} %select_n.21), kind=kOutput, calls=%fused_computation.63 | convolution fusion | flops 2562841600 | bytes 11453652 | tf_op jit(solution)/shard_map/td,fd->tf/dot_general | solution.py:147
  191.2 5.2 fusion.89
  196.5 7.5 convolution_convert_fusion
  204.1 40.4 %reduce-scatter.15.cloned.1.call-done = f32[256,1152]{1,0:T(8,128)} async-done(((f32[1024,1152]{1,0:T(8,128)}), f32[256,1152]{1,0:T(8,128)}) %reduce-scatter.15.cloned.1.call-update) | async-done | bytes 1179664 | tf_op jit(solution)/shard_map/reduce_scatter | solution.py:152
  244.5 2.4 multiply_reduce_fusion.1
  246.8 33.1 %reduce-scatter.13.cloned.1.call-done = bf16[256,1152]{1,0:T(8,128)(2,1)} async-done(((bf16[1024,1152]{1,0:T(8,128)(2,1)}), bf16[256,1152]{1,0:T(8,128)(2,1)}) %reduce-scatter.13.cloned.1.call-update) | async-done | bytes 589840 | tf_op jit(solution)/shard_map/reduce_scatter | solution.py:133
  280.0 3.6 fusion.84
  284.8 23.9 %all-gather.8.cloned.1.call-done = bf16[1024,1152]{1,0:T(8,128)(2,1)} async-done(((bf16[256,1152]{1,0:T(8,128)(2,1)}), bf16[1024,1152]{1,0:T(8,128)(2,1)}) %all-gather.8.cloned.1.call-update) | async-done | bytes 2359312 | tf_op jit(solution)/shard_map/all_gather | solution.py:161
  308.8 3.6 convolution_convert_fusion.1
  316.4 25.9 %while.52 = (s32[]{:T(128)}, f32[1024,4,72]{0,2,1:T(8,128)S(1)}, f32[1024,4,72]{0,2,1:T(8,128)}, bf16[2,512,4,72]{1,3,2,0:T(8,128)(2,1)}, bf16[2,512,4,72]{1,3,2...) while((s32[]{:T(128)}, f32[1024,4,72]{0,2,1:T(8,128)S(1)}, ...), condition=%wide.region_16.17_spmd.clone, body=%wide.region_14.16_spmd.clone.sunk | while | flops 1543698432 | bytes 91916632 | solution.py:206
  318.2 2.6 fusion.149
  320.9 3.3 multiply_reduce_fusion.7
  324.2 2.4 multiply_convert_fusion.6
  331.0 2.6 fusion.149
  333.7 3.3 multiply_reduce_fusion.7
  337.0 2.4 multiply_convert_fusion.6
  344.9 6.3 convolution_bitcast_fusion.1
  351.2 8.6 %copy.41 = f32[3,1152,288]{2,0,1:T(4,128)} copy(f32[3,1152,288]{1,2,0:T(8,128)} %convolution_bitcast_fusion.1) | data formatting | bytes 7962624
  359.8 8.9 %reshape.211 = f32[1152,864]{1,0:T(8,128)} reshape(f32[1152,3,288]{2,1,0:T(4,128)} %bitcast.141) | data formatting | bytes 7962624
  370.4 6.3 convolution_bitcast_fusion
  376.8 8.7 %fusion.54 = f32[1076,1152]{0,1:T(8,128)} fusion(bf16[2048,1152]{1,0:T(8,128)(2,1)} %constant_dynamic-update-slice_fusion, s32[]{:T(128)S(6)} %select_n.21, f32[1024,1076]{0,1:T(8,128)} %copy-done.51), kind=kOutput, calls=%fused_computation.72 | convolution fusion | flops 2548518912 | bytes 11741188 | tf_op jit(solution)/shard_map/tf,td->fd/dot_general | solution.py:149
  385.8 8.0 fusion.91
  394.9 4.5 fusion.90
  399.4 22.0 %pmax.7 = f32[4]{0:T(128)S(1)} all-reduce(f32[4]{0:T(128)S(1)} %reduce_max.27), channel_id=1, replica_groups=mesh['dp'=8,'tensor'=4] {'dp'}, use_global_device_ids=true, to_apply=%region_37.38 | all-reduce | flops 4 | bytes 32 | tf_op jit(solution)/shard_map/pmax | solution.py:140
  424.1 34.2 %all-reduce = (f32[2,288]{1,0:T(2,128)}, f32[1076]{0:T(1024)}) all-reduce(f32[2,288]{1,0:T(2,128)S(1)} %pad_maximum_fusion.3, f32[1076]{0:T(1024)S(1)} %copy-done.44), channel_id=1, replica_groups=mesh['dp'=8,'tensor'=4] {'dp'}, use_global_device_ids=true, to_apply=%region_26.27 | all-reduce | flops 1652 | bytes 13216 | tf_op jit(solution)/shard_map/psum | solution.py:244
  458.3 2.4 reshape.212
  462.9 44.7 %reduce-scatter.17.cloned.1.call-done = f32[256,1152]{1,0:T(8,128)} async-done(((f32[1024,1152]{1,0:T(8,128)}), f32[256,1152]{1,0:T(8,128)}) %reduce-scatter.17.cloned.1.call-update) | async-done | bytes 1179664 | tf_op jit(solution)/shard_map/reduce_scatter | solution.py:229
  509.6 43.0 %psum.23 = f32[6,1152]{1,0:T(8,128)} all-reduce(f32[6,1152]{1,0:T(8,128)S(1)} %stack.43), channel_id=1, replica_groups=mesh['dp'=8,'tensor'=4] {'dp','tensor'}, use_global_device_ids=true, to_apply=%region_35.36 | all-reduce | flops 6912 | bytes 55296 | tf_op jit(solution)/shard_map/psum | solution.py:255
  552.5 2.9 fusion.75
  555.5 62.0 %reduce-scatter.23.cloned.1.call-done = f32[1076,144]{0,1:T(8,128)} async-done(((f32[1076,1152]{0,1:T(8,128)}), f32[1076,144]{0,1:T(8,128)}) %reduce-scatter.23.cloned.1.call-update) | async-done | bytes 619792 | tf_op jit(solution)/shard_map/reduce_scatter | solution.py:242
  617.5 108.0 %reduce-scatter.21.cloned.1.call-done = f32[144,1076]{1,0:T(8,128)} async-done(((f32[1152,1076]{1,0:T(8,128)}), f32[144,1076]{1,0:T(8,128)}) %reduce-scatter.21.cloned.1.call-update) | async-done | bytes 619792 | tf_op jit(solution)/shard_map/reduce_scatter | solution.py:241
  725.4 70.1 %reduce-scatter.19.cloned.1.call-done = f32[288,144]{0,1:T(8,128)} async-done(((f32[288,1152]{0,1:T(8,128)}), f32[288,144]{0,1:T(8,128)}) %reduce-scatter.19.cloned.1.call-update) | async-done | bytes 165904 | tf_op jit(solution)/shard_map/reduce_scatter | solution.py:240
  (234 shorter events, 59.4 us)
Async XLA Ops:
  7.2 172.4 %copy-start = (bf16[1076,1152]{1,0:T(8,128)(2,1)S(1)}, bf16[1076,1152]{1,0:T(8,128)(2,1)}, u32[]{:S(2)}) copy-start(bf16[1076,1152]{1,0:T(8,128)(2,1)} %param.31) | copy-start | bytes 7437316
  7.2 5.1 copy-start.28
  7.2 5.1 copy-start.45
  7.2 32.0 %all-gather.4.cloned.1.call-start = ((), (), s32[]{:S(2)}) async-start(), calls=%async_computation.8 | async-start | bytes 2949120 | tf_op jit(solution)/shard_map/all_gather | solution.py:81
  8.6 30.5 %copy-start.35 = (f32[256]{0:T(256)}, f32[256]{0:T(256)S(1)}, u32[]{:S(2)}) copy-start(f32[256]{0:T(256)S(1)} %broadcast_multiply_fusion.5) | copy-start | bytes 3076
  10.0 29.2 %copy-start.39 = (f32[256]{0:T(256)}, f32[256]{0:T(256)S(1)}, u32[]{:S(2)}) copy-start(f32[256]{0:T(256)S(1)} %add_rsqrt_fusion.1) | copy-start | bytes 3076
  12.2 115.5 %reduce-scatter.11.cloned.1.call-start = ((), (), s32[]{:S(2)}) async-start(), calls=%async_computation.9 | async-start | bytes 5898240 | tf_op jit(solution)/shard_map/reduce_scatter | solution.py:122
  12.4 31.6 %copy-start.37 = (f32[288]{0:T(512)}, f32[288]{0:T(512)S(1)}, u32[]{:S(2)}) copy-start(f32[288]{0:T(512)S(1)} %get-tuple-element.296) | copy-start | bytes 3460
  73.3 6.4 copy-start.46
  79.7 48.0 %copy-start.41 = (f32[1152]{0:T(1024)S(1)}, f32[1152]{0:T(1024)}, u32[]{:S(2)}) copy-start(f32[1152]{0:T(1024)} %param.26) | copy-start | bytes 13828
  79.7 50.7 %copy-start.29 = (f32[1152]{0:T(1024)S(1)}, f32[1152]{0:T(1024)}, u32[]{:S(2)}) copy-start(f32[1152]{0:T(1024)} %param.27) | copy-start | bytes 13828
  79.8 50.7 %copy-start.42 = (f32[1152]{0:T(1024)S(1)}, f32[1152]{0:T(1024)}, u32[]{:S(2)}) copy-start(f32[1152]{0:T(1024)} %param.28) | copy-start | bytes 13828
  79.8 94.3 %all-gather.6.cloned.1.call-start = ((), (), s32[]{:S(2)}) async-start(), calls=%async_computation.10 | async-start | bytes 2949120 | tf_op jit(solution)/shard_map/all_gather | solution.py:130
  79.8 51.8 %collective-permute-start = (bf16[256,1152]{1,0:T(8,128)(2,1)}, bf16[256,1152]{1,0:T(8,128)(2,1)}, u32[]{:S(2)}, u32[]{:S(2)}) collective-permute-start(bf16[256,1152]{1,0:T(8,128)(2,1)} %param.33), channel_id=1, source_target_pairs={{0,1},{1,2},{2,3},{3,0},{4,5},{5,6},{6,7},{7,4},{8,9},{9,10},{10,1... | collective-permute-start | bytes 1769480 | tf_op jit(solution)/shard_map/ppermute | solution.py:22
  131.5 112.9 %reduce-scatter.15.cloned.1.call-start = ((), (), s32[]{:S(2)}) async-start(), calls=%async_computation.12 | async-start | bytes 5898240 | tf_op jit(solution)/shard_map/reduce_scatter | solution.py:152
  131.6 9.7 %collective-permute-start.1 = (bf16[256,1152]{1,0:T(8,128)(2,1)}, bf16[256,1152]{1,0:T(8,128)(2,1)}, u32[]{:S(2)}, u32[]{:S(2)}) collective-permute-start(bf16[256,1152]{1,0:T(8,128)(2,1)} %collective-permute-done), channel_id=1, source_target_pairs={{0,1},{1,2},{2,3},{3,0},{4,5},{5,6},{6,7},{7,4},{8,9},{9,10},{10,1... | collective-permute-start | bytes 1769480 | tf_op jit(solution)/shard_map/ppermute | solution.py:22
  141.3 19.4 %collective-permute-start.2 = (bf16[256,1152]{1,0:T(8,128)(2,1)}, bf16[256,1152]{1,0:T(8,128)(2,1)}, u32[]{:S(2)}, u32[]{:S(2)}) collective-permute-start(bf16[256,1152]{1,0:T(8,128)(2,1)} %collective-permute-done.1), channel_id=1, source_target_pairs={{0,1},{1,2},{2,3},{3,0},{4,5},{5,6},{6,7},{7,4},{8,9},{9,10},{10,1... | collective-permute-start | bytes 1769480 | tf_op jit(solution)/shard_map/ppermute | solution.py:22
  141.5 25.0 %copy-start.10 = (bf16[256,1152]{1,0:T(8,128)(2,1)S(1)}, bf16[256,1152]{1,0:T(8,128)(2,1)}, u32[]{:S(2)}) copy-start(bf16[256,1152]{1,0:T(8,128)(2,1)} %param.33) | copy-start | bytes 1769476
  167.3 6.8 copy-start.49
  179.6 10.1 %copy-start.51 = (f32[1024,1076]{0,1:T(8,128)}, f32[1024,1076]{0,1:T(8,128)S(1)}, u32[]{:S(2)}) copy-start(f32[1024,1076]{0,1:T(8,128)S(1)} %convolution_add_fusion) | copy-start | bytes 13221892
  179.6 11.6 %copy-start.48 = (bf16[1152,1076]{0,1:T(8,128)(2,1)S(1)}, bf16[1152,1076]{0,1:T(8,128)(2,1)}, u32[]{:S(2)}) copy-start(bf16[1152,1076]{0,1:T(8,128)(2,1)} %param.29) | copy-start | bytes 7437316
  196.5 83.5 %reduce-scatter.13.cloned.1.call-start = ((), (), s32[]{:S(2)}) async-start(), calls=%async_computation.11 | async-start | bytes 2949120 | tf_op jit(solution)/shard_map/reduce_scatter | solution.py:133
  204.0 40.5 %copy-start.4 = (f32[256,1152]{1,0:T(8,128)S(1)}, f32[256,1152]{1,0:T(8,128)}, u32[]{:S(2)}) copy-start(f32[256,1152]{1,0:T(8,128)} %copy-done.3) | copy-start | bytes 3538948
  204.0 76.0 %copy-start.43 = (f32[1152]{0:T(1024)S(1)}, f32[1152]{0:T(1024)}, u32[]{:S(2)}) copy-start(f32[1152]{0:T(1024)} %param.32) | copy-start | bytes 13828
  204.0 104.8 %all-gather.8.cloned.1.call-start = ((), (), s32[]{:S(2)}) async-start(), calls=%async_computation.13 | async-start | bytes 2949120 | tf_op jit(solution)/shard_map/all_gather | solution.py:161
  283.6 25.2 %copy-start.8 = (f32[256,1152]{1,0:T(8,128)}, f32[256,1152]{1,0:T(8,128)S(1)}, u32[]{:S(2)}) copy-start(f32[256,1152]{1,0:T(8,128)S(1)} %get-tuple-element.340) | copy-start | bytes 3538948
  284.6 173.7 %reduce-scatter.25.cloned.1.call-start = ((), (), s32[]{:S(2)}) async-start(), calls=%async_computation.18 | async-start | bytes 4644864
  342.4 8.8 %copy-start.24 = (bf16[1024,4,72]{0,2,1:T(8,128)(2,1)}, bf16[1024,4,72]{0,2,1:T(8,128)(2,1)S(1)}, u32[]{:S(2)}) copy-start(bf16[1024,4,72]{0,2,1:T(8,128)(2,1)S(1)} %convert_element_type.109) | copy-start | bytes 1769476
  344.7 6.5 copy-start.26
  344.9 6.3 copy-start.27
  368.8 138.9 %reduce-scatter.17.cloned.1.call-start = ((), (), s32[]{:S(2)}) async-start(), calls=%async_computation.14 | async-start | bytes 5898240 | tf_op jit(solution)/shard_map/reduce_scatter | solution.py:229
  376.8 240.7 %reduce-scatter.23.cloned.1.call-start = ((), (), s32[]{:S(2)}) async-start(), calls=%async_computation.17 | async-start | bytes 5971968 | tf_op jit(solution)/shard_map/reduce_scatter | solution.py:242
  385.5 339.9 %reduce-scatter.21.cloned.1.call-start = ((), (), s32[]{:S(2)}) async-start(), calls=%async_computation.16 | async-start | bytes 5971968 | tf_op jit(solution)/shard_map/reduce_scatter | solution.py:241
  393.8 5.6 copy-start.47
  393.8 27.8 %copy-start.38 = (f32[288]{0:T(512)S(1)}, f32[288]{0:T(512)}, u32[]{:S(2)}) copy-start(f32[288]{0:T(512)} %copy-done.37) | copy-start | bytes 3460
  393.8 401.7 %reduce-scatter.19.cloned.1.call-start = ((), (), s32[]{:S(2)}) async-start(), calls=%async_computation.15 | async-start | bytes 1990656 | tf_op jit(solution)/shard_map/reduce_scatter | solution.py:240
  399.3 24.2 %copy-start.32 = (f32[1152]{0:T(1024)S(1)}, f32[1152]{0:T(1024)}, u32[]{:S(2)}) copy-start(f32[1152]{0:T(1024)} %get-tuple-element.287) | copy-start | bytes 13828
  399.3 24.3 %copy-start.34 = (f32[1152]{0:T(1024)S(1)}, f32[1152]{0:T(1024)}, u32[]{:S(2)}) copy-start(f32[1152]{0:T(1024)} %get-tuple-element.339) | copy-start | bytes 13828
  399.3 24.3 %copy-start.33 = (f32[1152]{0:T(1024)S(1)}, f32[1152]{0:T(1024)}, u32[]{:S(2)}) copy-start(f32[1152]{0:T(1024)} %get-tuple-element.352) | copy-start | bytes 13828
  399.4 24.3 %copy-start.31 = (f32[1152]{0:T(1024)S(1)}, f32[1152]{0:T(1024)}, u32[]{:S(2)}) copy-start(f32[1152]{0:T(1024)} %get-tuple-element.293) | copy-start | bytes 13828
  399.4 24.3 %copy-start.13 = (bf16[2,512,4,72]{1,3,2,0:T(8,128)(2,1)S(1)}, bf16[2,512,4,72]{1,3,2,0:T(8,128)(2,1)}, u32[]{:S(2)}) copy-start(bf16[2,512,4,72]{1,3,2,0:T(8,128)(2,1)} %get-tuple-element.176) | copy-start | bytes 1769476
  399.4 24.7 %copy-start.44 = (f32[1076]{0:T(1024)S(1)}, f32[1076]{0:T(1024)}, u32[]{:S(2)}) copy-start(f32[1076]{0:T(1024)} %get-tuple-element.353) | copy-start | bytes 12916
  421.5 39.3 %copy-start.50 = (f32[4]{0:T(128)}, f32[4]{0:T(128)S(1)}, u32[]{:S(2)}) copy-start(f32[4]{0:T(128)S(1)} %pmax.7) | copy-start | bytes 52
  423.6 84.1 %copy-start.7 = (bf16[256,1152]{1,0:T(8,128)(2,1)S(1)}, bf16[256,1152]{1,0:T(8,128)(2,1)}, u32[]{:S(2)}) copy-start(bf16[256,1152]{1,0:T(8,128)(2,1)} %param.19) | copy-start | bytes 1769476
  423.6 84.1 %copy-start.30 = (f32[1152]{0:T(1024)S(1)}, f32[1152]{0:T(1024)}, u32[]{:S(2)}) copy-start(f32[1152]{0:T(1024)} %param.21) | copy-start | bytes 13828
  423.6 84.1 %copy-start.36 = (f32[256]{0:T(256)S(1)}, f32[256]{0:T(256)}, u32[]{:S(2)}) copy-start(f32[256]{0:T(256)} %copy-done.35) | copy-start | bytes 3076
  423.6 84.1 %copy-start.40 = (f32[256]{0:T(256)S(1)}, f32[256]{0:T(256)}, u32[]{:S(2)}) copy-start(f32[256]{0:T(256)} %copy-done.39) | copy-start | bytes 3076
  460.7 334.8 %copy-start.1 = (bf16[1076,1152]{1,0:T(8,128)(2,1)S(1)}, bf16[1076,1152]{1,0:T(8,128)(2,1)}, u32[]{:S(2)}) copy-start(bf16[1076,1152]{1,0:T(8,128)(2,1)} %param.31) | copy-start | bytes 7437316
  (28 other events, 56.9 us)
Sparse Core Ops, SparseCore 0:
  12.4 26.7 all-gather.3
  79.9 47.8 reduce-scatter.10
  131.7 28.9 all-gather.5
  196.6 47.8 reduce-scatter.14
  246.8 33.0 reduce-scatter.12
  284.7 24.0 all-gather.7
  368.9 88.4 reduce-scatter.24
  459.9 47.7 reduce-scatter.16
  512.2 105.1 reduce-scatter.22
  621.5 103.9 reduce-scatter.20
  729.9 65.6 reduce-scatter.18
